TPU v7x, 32 devices: a whole 2x2x4 slice. The times are simulated.
32 devices in a mesh: task: 2 (over y), fsdp: 16 (over z, x, core).
Axes of the slice: x: 2, y: 2, z: 4, core: 2. Of those that a mesh axis runs over, the one named last changes fastest.
Arguments:
- contexts: bfloat16 [2, 3072, 4096], P('task', 'fsdp'), may hold values from -3400 to 3400
- cotangents: bfloat16 [2, 3072, 4096], P('task', 'fsdp'), may hold values from -3400 to 3400
- adapter: bfloat16 [4096, 256], P('fsdp'), may hold values from -0.09375 to 0.09375
- moment_one: float32 [4096, 256], P('fsdp', 'task'), may hold values from -6 to 6
- moment_two: float32 [4096, 256], P('fsdp', 'task'), may hold values from 0.01 to 10
Outputs:
- first_moment: float32 [4096, 256], P('fsdp', 'task')
- second_moment: float32 [4096, 256], P('fsdp', 'task')
- adam_step: float32 [4096, 256], P('fsdp', 'task')
All inputs are finite; a program needn't handle non-finite values.
Results may differ from a plain program's by a relative error of at most 0.0004.
The roundings to bfloat16 on the way count: a program that leaves them out, or rounds other values in their place, can miss the bound.
Values may be sent and summed in bfloat16 or wider, within the bound.
A program may use at most 64 MiB of HBM per device.

v0:
```python
import math

import jax
import jax.numpy as jnp
from jax import lax
from jax.sharding import PartitionSpec as P

D = 4096
RANK = 128


def eliminate(matrix, vector):
    extent = vector.shape[0]
    matrix_rows = [matrix[position] for position in range(extent)]
    values = [vector[position] for position in range(extent)]
    for column in range(extent):
        for target in range(column + 1, extent):
            factor = matrix_rows[target][column] / matrix_rows[column][column]
            matrix_rows[target] = matrix_rows[target] - factor * matrix_rows[column]
            values[target] = values[target] - factor * values[column]
    answer = [values[0] for position in range(extent)]
    for column in reversed(range(extent)):
        running = values[column]
        for follow in range(column + 1, extent):
            running = running - matrix_rows[column][follow] * answer[follow]
        answer[column] = running / matrix_rows[column][column]
    return jnp.stack(answer)


def task_weights(gram_matrix):
    task_norms = jnp.sqrt(jnp.diagonal(gram_matrix))
    right_side = gram_matrix[0, 0] / task_norms[0] - gram_matrix[0, 1:] / task_norms[1:]
    system = (gram_matrix[0, 0] - gram_matrix[1:, 0])[:, None] / task_norms[0] - (
        gram_matrix[0, 1:][None, :] - gram_matrix[1:, 1:]
    ) / task_norms[1:][None, :]
    solution = eliminate(system.T, right_side)
    return jnp.concatenate([jnp.reshape(1.0 - jnp.sum(solution), (1,)), solution])


def body(contexts, cotangents, adapter, moment_one, moment_two):
    own_context = contexts[0]
    own_cotangent = cotangents[0]
    rank_width = adapter.shape[1] // 2
    piece = lax.all_gather(adapter, "fsdp", axis=0, tiled=True)
    context_cols = own_context
    cotangent_cols = own_cotangent
    low_part = jnp.dot(context_cols, piece[:, :rank_width], preferred_element_type=jnp.float32)
    back_part = jnp.dot(cotangent_cols, piece[:, rank_width:], preferred_element_type=jnp.float32)
    low = low_part.astype(jnp.bfloat16)
    back = back_part.astype(jnp.bfloat16)
    context_cols = own_context
    cotangent_cols = own_cotangent
    down_part = lax.dot_general(
        context_cols, back, (((0,), (0,)), ((), ())), preferred_element_type=jnp.float32
    )
    up_part = lax.dot_general(
        cotangent_cols, low, (((0,), (0,)), ((), ())), preferred_element_type=jnp.float32
    )
    grad_rows = lax.psum_scatter(
        jnp.concatenate([down_part, up_part], axis=1), "fsdp", scatter_dimension=0, tiled=True
    )
    gathered = lax.all_gather(grad_rows[None], "task", axis=0, tiled=True)
    partial_gram = jnp.einsum("sij,tij->st", gathered, gathered, precision=lax.Precision.HIGHEST)
    gram_matrix = lax.psum(partial_gram, "fsdp")
    block_width = gathered.shape[2] // lax.axis_size("task")
    pieces = lax.dynamic_slice_in_dim(
        gathered, lax.axis_index("task") * block_width, block_width, 2
    )
    task_alpha = task_weights(gram_matrix)
    combined = jnp.einsum("t,tij->ij", task_alpha, pieces, precision=lax.Precision.HIGHEST)
    squared = lax.psum(jnp.sum(combined * combined), ("task", "fsdp"))
    grad_norm = jnp.sqrt(1e-06 + squared)
    clipped = combined * (math.sqrt(2 * RANK * D) / grad_norm)
    first_moment = 0.9 * moment_one + 0.1 * clipped
    second_moment = 0.95 * moment_two + 0.05 * clipped * clipped
    adam_step = (
        first_moment / (1.0 - 0.9**20) / (jnp.sqrt(second_moment / (1.0 - 0.95**20)) + 1e-08)
    )
    return (first_moment, second_moment, adam_step)


def solution(mesh):
    in_specs = (
        P("task", "fsdp", None),
        P("task", "fsdp", None),
        P("fsdp", None),
        P("fsdp", "task"),
        P("fsdp", "task"),
    )
    out_specs = (P("fsdp", "task"), P("fsdp", "task"), P("fsdp", "task"))
    return jax.shard_map(body, mesh=mesh, in_specs=in_specs, out_specs=out_specs, check_vma=False)
```

profile of v0, /device:TPU:0, one launch (start us, length us, event | category | flops | bytes accessed | tf_op | source)
XLA Modules:
  0.0 236.0 jit_solution(14281167049697902435)
XLA Ops:
  7.2 0.0 copy-start
  7.2 0.0 all-gather.3.cloned.1.call-start
  7.2 0.7 all-gather.3.cloned.1.call-update
  7.9 0.0 copy-start.1
  7.9 0.0 reduce-scatter.2.cloned.1.call-start
  8.0 46.3 %all-gather.3.cloned.1.call-done = bf16[4096,256]{1,0:T(8,128)(2,1)} async-done(((bf16[256,256]{1,0:T(8,128)(2,1)}), bf16[4096,256]{1,0:T(8,128)(2,1)}) %all-gather.3.cloned.1.call-update) | async-done | bytes 2097168 | tf_op jit(solution)/shard_map/all_gather | solution.py:44
  54.3 0.0 copy-done
  54.3 4.1 %convolution_bitcast_fusion = f32[4096,128]{0,1:T(8,128)} fusion(bf16[1,192,4096]{2,1,0:T(8,128)(2,1)S(1)} %copy-done, bf16[1,192,4096]{2,1,0:T(8,128)(2,1)} %param.5, bf16[4096,256]{1,0:T(8,128)(2,1)} %all-gather.3.cloned.1.call-done), kind=kOutput, calls=%fused_computation.1 | convolution fusion | flops 402677760 | bytes 6291456 | tf_op jit(solution)/shard_map/dot_general | solution.py:56
  58.4 0.0 copy-done.1
  58.4 3.6 %convolution_bitcast_fusion.1 = f32[4096,128]{0,1:T(8,128)} fusion(bf16[1,192,4096]{2,1,0:T(8,128)(2,1)S(1)} %copy-done.1, bf16[1,192,4096]{2,1,0:T(8,128)(2,1)S(1)} %copy-done, bf16[4096,256]{1,0:T(8,128)(2,1)} %all-gather.3.cloned.1.call-done), kind=kOutput, calls=%fused_computation.2 | convolution fusion | flops 402677760 | bytes 6291456 | tf_op jit(solution)/shard_map/dot_general | solution.py:53
  61.9 4.6 %pad_maximum_fusion = f32[4096,256]{0,1:T(8,128)} fusion(f32[4096,128]{0,1:T(8,128)} %convolution_bitcast_fusion, f32[4096,128]{0,1:T(8,128)} %convolution_bitcast_fusion.1), kind=kLoop, calls=%fused_computation.3 | loop fusion | flops 1048576 | bytes 8388608 | tf_op jit(solution)/shard_map/concatenate | solution.py:60
  66.5 0.0 reduce-scatter.2.cloned.1.call-update
  66.6 71.4 %reduce-scatter.2.cloned.1.call-done = f32[256,256]{0,1:T(8,128)} async-done(((f32[4096,256]{0,1:T(8,128)}), f32[256,256]{0,1:T(8,128)}) %reduce-scatter.2.cloned.1.call-update) | async-done | bytes 262160 | tf_op jit(solution)/shard_map/reduce_scatter | solution.py:59
  138.0 7.3 %all-gather = f32[512,256]{0,1:T(8,128)S(1)} all-gather(f32[256,256]{0,1:T(8,128)} %reduce-scatter.2.cloned.1.call-done), channel_id=2, replica_groups=mesh['task'=2,'fsdp'=16] {'task'}, dimensions={0}, use_global_device_ids=true | all-gather | bytes 786432 | tf_op jit(solution)/shard_map/all_gather | solution.py:62
  145.3 0.0 copy-start.2
  145.3 0.0 copy-start.3
  145.3 0.3 reshape.20
  145.6 4.9 %convolution_bitcast_fusion.2 = f32[2,2]{1,0:T(2,128)S(1)} fusion(f32[2,256,256]{1,0,2:T(2,128)S(1)} %reshape.20), kind=kOutput, calls=%fused_computation.12 | convolution fusion | flops 3145728 | bytes 524304 | tf_op jit(solution)/shard_map/sij,tij->st/dot_general | solution.py:63
  150.5 29.9 %psum.14 = f32[2,2]{1,0:T(2,128)S(1)} all-reduce(f32[2,2]{1,0:T(2,128)S(1)} %convolution_bitcast_fusion.2), channel_id=1, replica_groups=mesh['task'=2,'fsdp'=16] {'fsdp'}, use_global_device_ids=true, to_apply=%region_1.0 | all-reduce | flops 4 | bytes 32 | tf_op jit(solution)/shard_map/psum | solution.py:64
  180.4 0.6 fusion.29
  181.0 0.6 gather_fusion
  181.6 0.6 fusion.30
  188.8 1.0 fusion.20
  189.8 0.1 copy.14
  189.9 0.6 fusion.23
  190.6 37.1 %psum.15 = f32[]{:T(128)} all-reduce(f32[]{:T(128)} %fusion.23), channel_id=1, replica_groups=mesh['task'=2,'fsdp'=16] {'task','fsdp'}, use_global_device_ids=true, to_apply=%region_3.4 | all-reduce | flops 1 | bytes 8 | tf_op jit(solution)/shard_map/psum | solution.py:71
  228.3 0.0 copy-done.2
  228.3 0.0 copy-done.3
  228.4 0.8 add_divide_fusion
  (2 shorter events, 0.0 us)
Async XLA Ops:
  7.2 47.1 %copy-start = (bf16[1,192,4096]{2,1,0:T(8,128)(2,1)S(1)}, bf16[1,192,4096]{2,1,0:T(8,128)(2,1)}, u32[]{:S(2)}) copy-start(bf16[1,192,4096]{2,1,0:T(8,128)(2,1)} %param.6) | copy-start | bytes 4718596
  7.2 47.1 %all-gather.3.cloned.1.call-start = ((), (), s32[]{:S(2)}) async-start(), calls=%async_computation.1 | async-start | bytes 2228224 | tf_op jit(solution)/shard_map/all_gather | solution.py:44
  7.9 50.5 %copy-start.1 = (bf16[1,192,4096]{2,1,0:T(8,128)(2,1)S(1)}, bf16[1,192,4096]{2,1,0:T(8,128)(2,1)}, u32[]{:S(2)}) copy-start(bf16[1,192,4096]{2,1,0:T(8,128)(2,1)} %param.5) | copy-start | bytes 4718596
  7.9 130.0 %reduce-scatter.2.cloned.1.call-start = ((), (), s32[]{:S(2)}) async-start(), calls=%async_computation.2 | async-start | bytes 4456448 | tf_op jit(solution)/shard_map/reduce_scatter | solution.py:59
  145.3 83.1 %copy-start.2 = (f32[256,128]{1,0:T(8,128)S(1)}, f32[256,128]{1,0:T(8,128)}, u32[]{:S(2)}) copy-start(f32[256,128]{1,0:T(8,128)} %param.9) | copy-start | bytes 393220
  145.3 83.1 %copy-start.3 = (f32[256,128]{1,0:T(8,128)S(1)}, f32[256,128]{1,0:T(8,128)}, u32[]{:S(2)}) copy-start(f32[256,128]{1,0:T(8,128)} %param.8) | copy-start | bytes 393220
Sparse Core Ops, SparseCore 0:
  10.2 44.0 all-gather.2
  66.7 71.2 reduce-scatter.1
where the time goes:
time: 237 us; the launch traced here: 236 us
  waiting for transfers between devices  118 us (50%)
  blocking collectives  74.2 us (31%)
  between operations  21.3 us (9%)
  matrix products  13.6 us (6%)
  other arithmetic  6.04 us (3%)
    reduce_scatter x1, waiting for transfers between devices, body(): lax.psum_scatter(jnp.concatenate([down_part, up_part], axis=1), 'fsdp', s...  71.4 us
    all_gather x1, waiting for transfers between devices, body(): piece = lax.all_gather(adapter, 'fsdp', axis=0, tiled=True)  46.3 us
    psum x1, blocking collectives, body(): squared = lax.psum(jnp.sum(combined * combined), ('task', 'fsdp'))  37.1 us
    psum x1, blocking collectives, body(): gram_matrix = lax.psum(partial_gram, 'fsdp')  29.9 us
    all_gather x1, blocking collectives, body(): gathered = lax.all_gather(grad_rows[None], 'task', axis=0, tiled=True)  7.28 us
    dot_general x1, matrix products, body(): jnp.einsum('sij,tij->st', gathered, gathered, precision=lax.Precision.HIG...  4.9 us
  transfers between devices with their start and end apart: 2, of which 2 were waited for; matrix products, arithmetic and copies ran while one was open for 0% of the time, Pallas kernels for 0%

commit v1 on v0

--- a/solution.py
+++ b/solution.py
@@ -3,10 +3,13 @@
 import jax
 import jax.numpy as jnp
 from jax import lax
+from jax.experimental import pallas as pl
+from jax.experimental.pallas import tpu as pltpu
 from jax.sharding import PartitionSpec as P
 
 D = 4096
 RANK = 128
+MESH = pl.DeviceIdType.MESH
 
 
 def eliminate(matrix, vector):
@@ -37,25 +40,27 @@
     return jnp.concatenate([jnp.reshape(1.0 - jnp.sum(solution), (1,)), solution])
 
 
-def body(contexts, cotangents, adapter, moment_one, moment_two):
+def adam(clipped, moment_one, moment_two):
+    first_moment = 0.9 * moment_one + 0.1 * clipped
+    second_moment = 0.95 * moment_two + 0.05 * clipped * clipped
+    adam_step = (
+        first_moment / (1.0 - 0.9**20) / (jnp.sqrt(second_moment / (1.0 - 0.95**20)) + 1e-08)
+    )
+    return (first_moment, second_moment, adam_step)
+
+
+def general_body(contexts, cotangents, adapter, moment_one, moment_two):
     own_context = contexts[0]
     own_cotangent = cotangents[0]
     rank_width = adapter.shape[1] // 2
     piece = lax.all_gather(adapter, "fsdp", axis=0, tiled=True)
-    context_cols = own_context
-    cotangent_cols = own_cotangent
-    low_part = jnp.dot(context_cols, piece[:, :rank_width], preferred_element_type=jnp.float32)
-    back_part = jnp.dot(cotangent_cols, piece[:, rank_width:], preferred_element_type=jnp.float32)
-    low = low_part.astype(jnp.bfloat16)
-    back = back_part.astype(jnp.bfloat16)
-    context_cols = own_context
-    cotangent_cols = own_cotangent
-    down_part = lax.dot_general(
-        context_cols, back, (((0,), (0,)), ((), ())), preferred_element_type=jnp.float32
-    )
-    up_part = lax.dot_general(
-        cotangent_cols, low, (((0,), (0,)), ((), ())), preferred_element_type=jnp.float32
-    )
+    low = jnp.dot(own_context, piece[:, :rank_width], preferred_element_type=jnp.float32)
+    back = jnp.dot(own_cotangent, piece[:, rank_width:], preferred_element_type=jnp.float32)
+    low = low.astype(jnp.bfloat16)
+    back = back.astype(jnp.bfloat16)
+    over_tokens = (((0,), (0,)), ((), ()))
+    down_part = lax.dot_general(own_context, back, over_tokens, preferred_element_type=jnp.float32)
+    up_part = lax.dot_general(own_cotangent, low, over_tokens, preferred_element_type=jnp.float32)
     grad_rows = lax.psum_scatter(
         jnp.concatenate([down_part, up_part], axis=1), "fsdp", scatter_dimension=0, tiled=True
     )
@@ -71,12 +76,238 @@
     squared = lax.psum(jnp.sum(combined * combined), ("task", "fsdp"))
     grad_norm = jnp.sqrt(1e-06 + squared)
     clipped = combined * (math.sqrt(2 * RANK * D) / grad_norm)
-    first_moment = 0.9 * moment_one + 0.1 * clipped
-    second_moment = 0.95 * moment_two + 0.05 * clipped * clipped
-    adam_step = (
-        first_moment / (1.0 - 0.9**20) / (jnp.sqrt(second_moment / (1.0 - 0.95**20)) + 1e-08)
-    )
-    return (first_moment, second_moment, adam_step)
+    return adam(clipped, moment_one, moment_two)
+
+
+def flip2(z, d):
+    if d == 0:
+        return z
+    if d == 1:
+        return z + 1 - 2 * (z % 2)
+    if d == 2:
+        return (z + 2) % 4
+    return 3 - z
+
+
+def kernel(
+    ctx, cot, ada, out,
+    gathered, grad, core_in, x_in, z_in, y_in, gram_out, gram_in, gram_mid, gram_last,
+    az_s, az_r, ax_s, ax_r, ac_s, ac_r,
+    gc_s, gc_r, gx_s, gx_r, gz_s, gz_r, gy_s, gy_r, ka_s, ka_r, kz_s, kz_r,
+):
+    f32 = jnp.float32
+    rows, width = ada.shape
+    rank = width // 2
+    t = lax.axis_index("task")
+    f = lax.axis_index("fsdp")
+    c = f % 2
+    x = (f // 2) % 2
+    z = f // 4
+
+    def place(z_, x_, c_):
+        return (z_ * 2 + x_) * 2 + c_
+
+    zpeer = {d: (t, place(flip2(z, d), x, c)) for d in (1, 2, 3)}
+    xpeer = (t, place(z, 1 - x, c))
+    cpeer = (t, place(z, x, 1 - c))
+    cube = {
+        k: (
+            1 - t if k & 4 else t,
+            place(z, 1 - x if k & 2 else x, 1 - c if k & 1 else c),
+        )
+        for k in range(1, 8)
+    }
+
+    def remote(src, dst, send, recv, peer):
+        return pltpu.make_async_remote_copy(
+            src_ref=src, dst_ref=dst, send_sem=send, recv_sem=recv, device_id=peer, device_id_type=MESH
+        )
+
+    barrier = pltpu.get_barrier_semaphore()
+    for peer in list(zpeer.values()) + list(cube.values()):
+        pl.semaphore_signal(barrier, inc=1, device_id=peer, device_id_type=MESH)
+    gathered[f] = ada[...]
+    pl.semaphore_wait(barrier, 10)
+
+    sent = []
+
+    def go(src, dst, send, recv, peer):
+        copy = remote(src, dst, send, recv, peer)
+        copy.start()
+        sent.append(copy)
+
+    def move_block(slot, send, recv, peer):
+        go(gathered.at[slot], gathered.at[slot], send, recv, peer)
+
+    def await_block(slot, send, recv, peer):
+        remote(gathered.at[slot], gathered.at[slot], send, recv, peer).wait_recv()
+
+    low = jnp.zeros((ctx.shape[0], rank), f32)
+    back = jnp.zeros((ctx.shape[0], rank), f32)
+
+    def columns(slot):
+        return pl.ds(pl.multiple_of(slot * rows, rows), rows)
+
+    def consume(slot, low, back):
+        cols = columns(slot)
+        low = low + jnp.dot(ctx[:, cols], gathered[slot, :, :rank], preferred_element_type=f32)
+        back = back + jnp.dot(cot[:, cols], gathered[slot, :, rank:], preferred_element_type=f32)
+        return low, back
+
+    for d in (3, 2, 1):
+        move_block(f, az_s.at[d], az_r.at[d], zpeer[d])
+    move_block(f, ax_s.at[0], ax_r.at[0], xpeer)
+    move_block(f, ac_s.at[0], ac_r.at[0], cpeer)
+    low, back = consume(f, low, back)
+    for d in (1, 2, 3):
+        slot = place(flip2(z, d), x, c)
+        await_block(slot, az_s.at[d], az_r.at[d], zpeer[d])
+        move_block(slot, ax_s.at[d], ax_r.at[d], xpeer)
+        move_block(slot, ac_s.at[d], ac_r.at[d], cpeer)
+        low, back = consume(slot, low, back)
+    for d in range(4):
+        slot = place(flip2(z, d), 1 - x, c)
+        await_block(slot, ax_s.at[d], ax_r.at[d], xpeer)
+        move_block(slot, ac_s.at[4 + d], ac_r.at[4 + d], cpeer)
+        low, back = consume(slot, low, back)
+    for k in range(8):
+        slot = place(flip2(z, k % 4), x if k < 4 else 1 - x, 1 - c)
+        await_block(slot, ac_s.at[k], ac_r.at[k], cpeer)
+        low, back = consume(slot, low, back)
+
+    low_t = low.T.astype(jnp.bfloat16)
+    back_t = back.T.astype(jnp.bfloat16)
+
+    def make(slot):
+        cols = columns(slot)
+        grad[slot, :rank, :] = jnp.dot(back_t, ctx[:, cols], preferred_element_type=f32)
+        grad[slot, rank:, :] = jnp.dot(low_t, cot[:, cols], preferred_element_type=f32)
+
+    order = (3, 2, 1, 0)
+
+    def to_core(d, far):
+        slot = place(flip2(z, d), 1 - x if far else x, 1 - c)
+        make(slot)
+        k = 4 * far + d
+        go(grad.at[slot], core_in.at[k], gc_s.at[k], gc_r.at[k], cpeer)
+
+    def keep(d, far):
+        make(place(flip2(z, d), 1 - x if far else x, c))
+
+    def add_core(d, far):
+        slot = place(flip2(z, d), 1 - x if far else x, c)
+        k = 4 * far + d
+        remote(core_in.at[k], core_in.at[k], gc_s.at[k], gc_r.at[k], cpeer).wait_recv()
+        grad[slot] = grad[slot] + core_in[k]
+        return slot
+
+    def to_x(d):
+        slot = add_core(d, 1)
+        go(grad.at[slot], x_in.at[d], gx_s.at[d], gx_r.at[d], xpeer)
+
+    to_core(order[0], 1)
+    keep(order[0], 1)
+    for before, now in zip(order[:-1], order[1:]):
+        to_core(now, 1)
+        to_x(before)
+        keep(now, 1)
+    to_x(order[-1])
+    for d in order:
+        to_core(d, 0)
+        keep(d, 0)
+    for d in order:
+        slot = add_core(d, 0)
+        remote(x_in.at[d], x_in.at[d], gx_s.at[d], gx_r.at[d], xpeer).wait_recv()
+        grad[slot] = grad[slot] + x_in[d]
+        if d:
+            go(grad.at[slot], z_in.at[d - 1], gz_s.at[d], gz_r.at[d], zpeer[d])
+    for d in (3, 2, 1):
+        remote(z_in.at[d - 1], z_in.at[d - 1], gz_s.at[d], gz_r.at[d], zpeer[d]).wait_recv()
+    mine = pl.ds(pl.multiple_of(t * rank, rank), rank)
+    theirs = pl.ds(pl.multiple_of((1 - t) * rank, rank), rank)
+    for wait in sent:
+        wait.wait_send()
+    sent.clear()
+    z_in[0, theirs, :] = grad[f, theirs, :] + z_in[0, theirs, :] + z_in[1, theirs, :] + z_in[2, theirs, :]
+    go(z_in.at[0, theirs, :], y_in, gy_s, gy_r, cube[4])
+    own = grad[f, mine, :] + z_in[0, mine, :] + z_in[1, mine, :] + z_in[2, mine, :]
+    remote(y_in, y_in, gy_s, gy_r, cube[4]).wait_recv()
+    other = y_in[...]
+
+    first = t == 0
+    own_sum = jnp.sum(own * own, axis=0, keepdims=True)
+    both_sum = jnp.sum(own * other, axis=0, keepdims=True)
+    other_sum = jnp.sum(other * other, axis=0, keepdims=True)
+    rows_list = [jnp.where(first, own_sum, other_sum), both_sum, jnp.where(first, other_sum, own_sum)]
+    gram_out[...] = jnp.zeros_like(gram_out)
+    for k in range(3):
+        total = rows_list[k]
+        acc = total[:, :128]
+        for j in range(1, rows // 128):
+            acc = acc + total[:, j * 128 : (j + 1) * 128]
+        gram_out[k : k + 1, :] = acc
+    corner = (t * 2 + x) * 2 + c
+    for k in range(1, 8):
+        go(gram_out, gram_in.at[corner], ka_s.at[k], ka_r.at[k], cube[k])
+    gram_in[corner] = gram_out[...]
+    for k in range(1, 8):
+        there = ((1 - t if k & 4 else t) * 2 + (1 - x if k & 2 else x)) * 2 + (1 - c if k & 1 else c)
+        remote(gram_out, gram_in.at[there], ka_s.at[k], ka_r.at[k], cube[k]).wait_recv()
+    gram_mid[...] = jnp.sum(gram_in[...], axis=0)
+    for d in (3, 2, 1):
+        go(gram_mid, gram_last.at[z], kz_s.at[d], kz_r.at[d], zpeer[d])
+    gram_last[z] = gram_mid[...]
+    for d in (3, 2, 1):
+        remote(gram_mid, gram_last.at[flip2(z, d)], kz_s.at[d], kz_r.at[d], zpeer[d]).wait_recv()
+    tile = jnp.sum(gram_last[...], axis=0)
+    sums = jnp.sum(tile, axis=1, keepdims=True)
+    k00, k01, k11 = sums[0:1], sums[1:2], sums[2:3]
+    n0, n1 = jnp.sqrt(k00), jnp.sqrt(k11)
+    right_side = k00 / n0 - k01 / n1
+    system = (k00 - k01) / n0 - (k01 - k11) / n1
+    alpha1 = right_side / system
+    alpha0 = 1.0 - alpha1
+    squared = alpha0 * alpha0 * k00 + 2.0 * alpha0 * alpha1 * k01 + alpha1 * alpha1 * k11
+    scale = math.sqrt(2 * RANK * D) / jnp.sqrt(1e-06 + jnp.maximum(squared, 0.0))
+    own_alpha = jnp.where(first, alpha0, alpha1) * scale
+    other_alpha = jnp.where(first, alpha1, alpha0) * scale
+    out[...] = (own * own_alpha + other * other_alpha).T
+    for wait in sent:
+        wait.wait_send()
+
+
+def kernel_body(contexts, cotangents, adapter, moment_one, moment_two):
+    rows, width = adapter.shape
+    rank = width // 2
+    f32 = jnp.float32
+    dma = pltpu.SemaphoreType.DMA
+    vmem = pl.BlockSpec(memory_space=pltpu.VMEM)
+    clipped = pl.pallas_call(
+        kernel,
+        out_shape=jax.ShapeDtypeStruct((rows, rank), f32),
+        in_specs=[vmem] * 3,
+        out_specs=vmem,
+        scratch_shapes=[
+            pltpu.VMEM((16, rows, width), adapter.dtype),
+            pltpu.VMEM((16, width, rows), f32),
+            pltpu.VMEM((8, width, rows), f32),
+            pltpu.VMEM((4, width, rows), f32),
+            pltpu.VMEM((3, width, rows), f32),
+            pltpu.VMEM((rank, rows), f32),
+            pltpu.VMEM((8, 128), f32),
+            pltpu.VMEM((8, 8, 128), f32),
+            pltpu.VMEM((8, 128), f32),
+            pltpu.VMEM((4, 8, 128), f32),
+            dma((4,)), dma((4,)), dma((4,)), dma((4,)), dma((8,)), dma((8,)),
+            dma((8,)), dma((8,)), dma((4,)), dma((4,)), dma((4,)), dma((4,)),
+            dma, dma, dma((8,)), dma((8,)), dma((4,)), dma((4,)),
+        ],
+        compiler_params=pltpu.CompilerParams(
+            collective_id=0, has_side_effects=True, vmem_limit_bytes=40 * 1024 * 1024
+        ),
+        name="grads_and_weights",
+    )(contexts[0], cotangents[0], adapter)
+    return adam(clipped, moment_one, moment_two)
 
 
 def solution(mesh):
@@ -88,4 +319,6 @@
         P("fsdp", "task"),
     )
     out_specs = (P("fsdp", "task"), P("fsdp", "task"), P("fsdp", "task"))
+    small = mesh.shape["task"] == 2 and mesh.shape["fsdp"] == 16
+    body = kernel_body if small else general_body
     return jax.shard_map(body, mesh=mesh, in_specs=in_specs, out_specs=out_specs, check_vma=False)

time: 237 us -> 78.7 us (0.33)
  waiting for transfers between devices: 118 us -> 0 us
  blocking collectives: 74.2 us -> 0 us
  Pallas kernels: 0 us -> 73.3 us
  between operations: 21.3 us -> 0.67 us
  matrix products: 13.6 us -> 0 us
  other arithmetic: 6.04 us -> 0.78 us
    pallas_call x0 -> x1, Pallas kernels: none -> 73.3 us  [kernel_body(): pl.pallas_call(kernel, out_shape=jax.ShapeDtypeStruct((rows, rank), f32),...]
    reduce_scatter x1 -> x0, waiting for transfers between devices: 71.4 us -> none  [body(): lax.psum_scatter(jnp.concatenate([down_part, up_part], axis=1), 'fsdp', s...]
    psum x2 -> x0, blocking collectives: 67 us -> none  [the longest x1 37.1 us: body(): squared = lax.psum(jnp.sum(combined * combined), ('task', 'fsdp'))]
    all_gather x1 -> x0, waiting for transfers between devices: 46.3 us -> none  [body(): piece = lax.all_gather(adapter, 'fsdp', axis=0, tiled=True)]
    dot_general x4 -> x0, matrix products: 13.6 us -> none  [the longest x1 4.9 us: body(): jnp.einsum('sij,tij->st', gathered, gathered, precision=lax.Precision.HIG...]
    all_gather x1 -> x0, blocking collectives: 7.28 us -> none  [body(): gathered = lax.all_gather(grad_rows[None], 'task', axis=0, tiled=True)]
    concatenate x2 -> x0, other arithmetic: 4.62 us -> none  [the longest x1 4.61 us: body(): jnp.concatenate([down_part, up_part], axis=1)]
    unnamed x8 -> x10, local copies, waits for them, and re-layouts: 0.02 us -> 3.72 us
  transfers between devices with their start and end apart: 2 -> 0, of which waited for: 2 -> 0; matrix products, arithmetic and copies ran while one was open for 0% -> 0% of each run, Pallas kernels for 0% -> 0%
where the time goes in v1:
time: 78.7 us; the launch traced here: 78.5 us
  Pallas kernels  73.3 us (93%)
  local copies, waits for them, and re-layouts  3.72 us (5%)
    pallas_call x1, Pallas kernels, kernel_body(): pl.pallas_call(kernel, out_shape=jax.ShapeDtypeStruct((rows, rank), f32),...  73.3 us
    unnamed x10, local copies, waits for them, and re-layouts  3.72 us

profile of v1, /device:TPU:0, one launch (start us, length us, event | category | flops | bytes accessed | tf_op | source)
XLA Modules:
  0.0 78.5 jit_solution(13193637293283338773)
XLA Ops:
  0.6 0.0 copy-start
  0.6 1.4 %copy-done = bf16[1,192,4096]{2,1,0:T(8,128)(2,1)S(1)} copy-done((bf16[1,192,4096]{2,1,0:T(8,128)(2,1)S(1)}, bf16[1,192,4096]{2,1,0:T(8,128)(2,1)}, u32[]{:S(2)}) %copy-start) | copy-done | bytes 1572888
  2.0 0.0 copy-start.1
  2.0 1.4 %copy-done.1 = bf16[1,192,4096]{2,1,0:T(8,128)(2,1)S(1)} copy-done((bf16[1,192,4096]{2,1,0:T(8,128)(2,1)S(1)}, bf16[1,192,4096]{2,1,0:T(8,128)(2,1)}, u32[]{:S(2)}) %copy-start.1) | copy-done | bytes 1572888
  3.4 0.0 copy-start.2
  3.5 0.9 %copy-done.2 = bf16[256,256]{1,0:T(8,128)(2,1)S(1)} copy-done((bf16[256,256]{1,0:T(8,128)(2,1)S(1)}, bf16[256,256]{1,0:T(8,128)(2,1)}, u32[]{:S(2)}) %copy-start.2) | copy-done | bytes 131096
  4.4 0.0 copy-start.3
  4.4 0.0 copy-start.4
  4.4 73.3 %grads_and_weights.1 = f32[256,128]{1,0:T(8,128)S(1)} custom-call(bf16[192,4096]{1,0:T(8,128)(2,1)S(1)} %bitcast.2, bf16[192,4096]{1,0:T(8,128)(2,1)S(1)} %bitcast.3, bf16[256,256]{1,0:T(8,128)(2,1)S(1)} %copy-done.2), custom_call_target="tpu_custom_call" | custom-call | tf_op jit(solution)/shard_map/grads_and_weights/pallas_call | solution.py:285
  77.7 0.0 copy-done.3
  77.7 0.0 copy-done.4
  77.7 0.8 add_divide_fusion
Async XLA Ops:
  0.6 1.4 %copy-start = (bf16[1,192,4096]{2,1,0:T(8,128)(2,1)S(1)}, bf16[1,192,4096]{2,1,0:T(8,128)(2,1)}, u32[]{:S(2)}) copy-start(bf16[1,192,4096]{2,1,0:T(8,128)(2,1)} %param.5) | copy-start | bytes 4718596
  2.0 1.4 %copy-start.1 = (bf16[1,192,4096]{2,1,0:T(8,128)(2,1)S(1)}, bf16[1,192,4096]{2,1,0:T(8,128)(2,1)}, u32[]{:S(2)}) copy-start(bf16[1,192,4096]{2,1,0:T(8,128)(2,1)} %param.6) | copy-start | bytes 4718596
  3.4 0.9 %copy-start.2 = (bf16[256,256]{1,0:T(8,128)(2,1)S(1)}, bf16[256,256]{1,0:T(8,128)(2,1)}, u32[]{:S(2)}) copy-start(bf16[256,256]{1,0:T(8,128)(2,1)} %ada.1) | copy-start | bytes 393220
  4.4 73.3 %copy-start.3 = (f32[256,128]{1,0:T(8,128)S(1)}, f32[256,128]{1,0:T(8,128)}, u32[]{:S(2)}) copy-start(f32[256,128]{1,0:T(8,128)} %param.9) | copy-start | bytes 393220
  4.4 73.3 %copy-start.4 = (f32[256,128]{1,0:T(8,128)S(1)}, f32[256,128]{1,0:T(8,128)}, u32[]{:S(2)}) copy-start(f32[256,128]{1,0:T(8,128)} %param.8) | copy-start | bytes 393220

commit v2 on v1

--- a/solution.py
+++ b/solution.py
@@ -90,14 +90,16 @@
 
 
 def kernel(
-    ctx, cot, ada, out,
+    ctx_hbm, cot_hbm, ada_hbm, out,
+    ctx, cot,
     gathered, grad, core_in, x_in, z_in, y_in, gram_out, gram_in, gram_mid, gram_last,
-    az_s, az_r, ax_s, ax_r, ac_s, ac_r,
+    load, az_s, az_r, ax_s, ax_r, ay_s, ay_r, ac_s, ac_r,
     gc_s, gc_r, gx_s, gx_r, gz_s, gz_r, gy_s, gy_r, ka_s, ka_r, kz_s, kz_r,
 ):
     f32 = jnp.float32
-    rows, width = ada.shape
+    rows, width = ada_hbm.shape
     rank = width // 2
+    half = rows // 2
     t = lax.axis_index("task")
     f = lax.axis_index("fsdp")
     c = f % 2
@@ -123,10 +125,16 @@
             src_ref=src, dst_ref=dst, send_sem=send, recv_sem=recv, device_id=peer, device_id_type=MESH
         )
 
+    loads = [
+        pltpu.make_async_copy(ada_hbm, gathered.at[f], load.at[0]),
+        pltpu.make_async_copy(ctx_hbm, ctx, load.at[1]),
+        pltpu.make_async_copy(cot_hbm, cot, load.at[2]),
+    ]
+    for copy in loads:
+        copy.start()
     barrier = pltpu.get_barrier_semaphore()
     for peer in list(zpeer.values()) + list(cube.values()):
         pl.semaphore_signal(barrier, inc=1, device_id=peer, device_id_type=MESH)
-    gathered[f] = ada[...]
     pl.semaphore_wait(barrier, 10)
 
     sent = []
@@ -136,11 +144,17 @@
         copy.start()
         sent.append(copy)
 
-    def move_block(slot, send, recv, peer):
-        go(gathered.at[slot], gathered.at[slot], send, recv, peer)
-
-    def await_block(slot, send, recv, peer):
-        remote(gathered.at[slot], gathered.at[slot], send, recv, peer).wait_recv()
+    near_half = pl.ds(pl.multiple_of(t * half, half), half)
+    far_half = pl.ds(pl.multiple_of((1 - t) * half, half), half)
+    whole = pl.ds(0, rows)
+    ypeer = cube[4]
+
+    def move_block(slot, part, send, recv, peer):
+        go(gathered.at[slot, part, :], gathered.at[slot, part, :], send, recv, peer)
+
+    def await_block(slot, part, send, recv, peer):
+        ref = gathered.at[slot, part, :]
+        remote(ref, ref, send, recv, peer).wait_recv()
 
     low = jnp.zeros((ctx.shape[0], rank), f32)
     back = jnp.zeros((ctx.shape[0], rank), f32)
@@ -154,26 +168,57 @@
         back = back + jnp.dot(cot[:, cols], gathered[slot, :, rank:], preferred_element_type=f32)
         return low, back
 
+    def line(d, far):
+        return place(flip2(z, d), 1 - x if far else x, c)
+
+    def to_other_core(slot, part, k):
+        move_block(slot, part, ac_s.at[k], ac_r.at[k], cpeer)
+
+    loads[0].wait()
     for d in (3, 2, 1):
-        move_block(f, az_s.at[d], az_r.at[d], zpeer[d])
-    move_block(f, ax_s.at[0], ax_r.at[0], xpeer)
-    move_block(f, ac_s.at[0], ac_r.at[0], cpeer)
+        move_block(f, near_half, az_s.at[d], az_r.at[d], zpeer[d])
+    move_block(f, whole, ax_s.at[0], ax_r.at[0], xpeer)
+    to_other_core(f, whole, 0)
+    loads[1].wait()
+    loads[2].wait()
     low, back = consume(f, low, back)
+
+    def from_z(d):
+        slot = line(d, 0)
+        await_block(slot, near_half, az_s.at[d], az_r.at[d], zpeer[d])
+        move_block(slot, near_half, ax_s.at[d], ax_r.at[d], xpeer)
+        move_block(slot, near_half, ay_s.at[d], ay_r.at[d], ypeer)
+        to_other_core(slot, near_half, d)
+
+    from_z(1)
+    from_z(2)
+    await_block(line(0, 1), whole, ax_s.at[0], ax_r.at[0], xpeer)
+    to_other_core(line(0, 1), whole, 4)
+    from_z(3)
+    low, back = consume(line(0, 1), low, back)
     for d in (1, 2, 3):
-        slot = place(flip2(z, d), x, c)
-        await_block(slot, az_s.at[d], az_r.at[d], zpeer[d])
-        move_block(slot, ax_s.at[d], ax_r.at[d], xpeer)
-        move_block(slot, ac_s.at[d], ac_r.at[d], cpeer)
+        slot = line(d, 1)
+        await_block(slot, near_half, ax_s.at[d], ax_r.at[d], xpeer)
+        move_block(slot, near_half, ay_s.at[4 + d], ay_r.at[4 + d], ypeer)
+        to_other_core(slot, near_half, 4 + d)
+    for far in (0, 1):
+        slot = place(z, 1 - x if far else x, 1 - c)
+        await_block(slot, whole, ac_s.at[4 * far], ac_r.at[4 * far], cpeer)
         low, back = consume(slot, low, back)
-    for d in range(4):
-        slot = place(flip2(z, d), 1 - x, c)
-        await_block(slot, ax_s.at[d], ax_r.at[d], xpeer)
-        move_block(slot, ac_s.at[4 + d], ac_r.at[4 + d], cpeer)
-        low, back = consume(slot, low, back)
-    for k in range(8):
-        slot = place(flip2(z, k % 4), x if k < 4 else 1 - x, 1 - c)
-        await_block(slot, ac_s.at[k], ac_r.at[k], cpeer)
-        low, back = consume(slot, low, back)
+    for far in (0, 1):
+        for d in (1, 2, 3):
+            k = 4 * far + d
+            slot = line(d, far)
+            await_block(slot, far_half, ay_s.at[k], ay_r.at[k], ypeer)
+            to_other_core(slot, far_half, 8 + k)
+            low, back = consume(slot, low, back)
+    for far in (0, 1):
+        for d in (1, 2, 3):
+            k = 4 * far + d
+            slot = place(flip2(z, d), 1 - x if far else x, 1 - c)
+            await_block(slot, near_half, ac_s.at[k], ac_r.at[k], cpeer)
+            await_block(slot, far_half, ac_s.at[8 + k], ac_r.at[8 + k], cpeer)
+            low, back = consume(slot, low, back)
 
     low_t = low.T.astype(jnp.bfloat16)
     back_t = back.T.astype(jnp.bfloat16)
@@ -183,7 +228,7 @@
         grad[slot, :rank, :] = jnp.dot(back_t, ctx[:, cols], preferred_element_type=f32)
         grad[slot, rank:, :] = jnp.dot(low_t, cot[:, cols], preferred_element_type=f32)
 
-    order = (3, 2, 1, 0)
+    order = (2, 3, 1, 0)
 
     def to_core(d, far):
         slot = place(flip2(z, d), 1 - x if far else x, 1 - c)
@@ -219,18 +264,19 @@
         slot = add_core(d, 0)
         remote(x_in.at[d], x_in.at[d], gx_s.at[d], gx_r.at[d], xpeer).wait_recv()
         grad[slot] = grad[slot] + x_in[d]
-        if d:
-            go(grad.at[slot], z_in.at[d - 1], gz_s.at[d], gz_r.at[d], zpeer[d])
-    for d in (3, 2, 1):
-        remote(z_in.at[d - 1], z_in.at[d - 1], gz_s.at[d], gz_r.at[d], zpeer[d]).wait_recv()
+        if d in (1, 2):
+            go(grad.at[slot], z_in.at[d], gz_s.at[d], gz_r.at[d], zpeer[1])
+        if d == 3:
+            remote(z_in.at[2], z_in.at[2], gz_s.at[2], gz_r.at[2], zpeer[1]).wait_recv()
+            grad[slot] = grad[slot] + z_in[2]
+            go(grad.at[slot], z_in.at[0], gz_s.at[3], gz_r.at[3], zpeer[3])
+    remote(z_in.at[1], z_in.at[1], gz_s.at[1], gz_r.at[1], zpeer[1]).wait_recv()
+    remote(z_in.at[0], z_in.at[0], gz_s.at[3], gz_r.at[3], zpeer[3]).wait_recv()
     mine = pl.ds(pl.multiple_of(t * rank, rank), rank)
     theirs = pl.ds(pl.multiple_of((1 - t) * rank, rank), rank)
-    for wait in sent:
-        wait.wait_send()
-    sent.clear()
-    z_in[0, theirs, :] = grad[f, theirs, :] + z_in[0, theirs, :] + z_in[1, theirs, :] + z_in[2, theirs, :]
+    z_in[0, theirs, :] = grad[f, theirs, :] + z_in[0, theirs, :] + z_in[1, theirs, :]
     go(z_in.at[0, theirs, :], y_in, gy_s, gy_r, cube[4])
-    own = grad[f, mine, :] + z_in[0, mine, :] + z_in[1, mine, :] + z_in[2, mine, :]
+    own = grad[f, mine, :] + z_in[0, mine, :] + z_in[1, mine, :]
     remote(y_in, y_in, gy_s, gy_r, cube[4]).wait_recv()
     other = y_in[...]
 
@@ -285,9 +331,11 @@
     clipped = pl.pallas_call(
         kernel,
         out_shape=jax.ShapeDtypeStruct((rows, rank), f32),
-        in_specs=[vmem] * 3,
+        in_specs=[pl.BlockSpec(memory_space=pltpu.HBM)] * 3,
         out_specs=vmem,
         scratch_shapes=[
+            pltpu.VMEM(contexts.shape[1:], contexts.dtype),
+            pltpu.VMEM(contexts.shape[1:], contexts.dtype),
             pltpu.VMEM((16, rows, width), adapter.dtype),
             pltpu.VMEM((16, width, rows), f32),
             pltpu.VMEM((8, width, rows), f32),
@@ -298,7 +346,7 @@
             pltpu.VMEM((8, 8, 128), f32),
             pltpu.VMEM((8, 128), f32),
             pltpu.VMEM((4, 8, 128), f32),
-            dma((4,)), dma((4,)), dma((4,)), dma((4,)), dma((8,)), dma((8,)),
+            dma((3,)), dma((4,)), dma((4,)), dma((4,)), dma((4,)), dma((8,)), dma((8,)), dma((16,)), dma((16,)),
             dma((8,)), dma((8,)), dma((4,)), dma((4,)), dma((4,)), dma((4,)),
             dma, dma, dma((8,)), dma((8,)), dma((4,)), dma((4,)),
         ],

time: 78.7 us -> 70.5 us (0.90)
  Pallas kernels: 73.3 us -> 65.1 us
    pallas_call x1, Pallas kernels: 73.3 us -> 65.1 us  [kernel_body(): pl.pallas_call(kernel, out_shape=jax.ShapeDtypeStruct((rows, rank), f32),...]
where the time goes in v2:
time: 70.5 us; the launch traced here: 70.3 us
  Pallas kernels  65.1 us (92%)
  local copies, waits for them, and re-layouts  3.72 us (5%)
  other arithmetic  0.78 us (1%)
    pallas_call x1, Pallas kernels, kernel_body(): pl.pallas_call(kernel, out_shape=jax.ShapeDtypeStruct((rows, rank), f32),...  65.1 us
    unnamed x10, local copies, waits for them, and re-layouts  3.72 us

profile of v2, /device:TPU:0, one launch (start us, length us, event | category | flops | bytes accessed | tf_op | source)
XLA Modules:
  0.0 70.3 jit_solution(3181353299405795847)
XLA Ops:
  0.6 0.0 copy-start
  0.6 1.4 %copy-done = bf16[1,192,4096]{2,1,0:T(8,128)(2,1)S(1)} copy-done((bf16[1,192,4096]{2,1,0:T(8,128)(2,1)S(1)}, bf16[1,192,4096]{2,1,0:T(8,128)(2,1)}, u32[]{:S(2)}) %copy-start) | copy-done | bytes 1572888
  2.0 0.0 copy-start.1
  2.0 1.4 %copy-done.1 = bf16[1,192,4096]{2,1,0:T(8,128)(2,1)S(1)} copy-done((bf16[1,192,4096]{2,1,0:T(8,128)(2,1)S(1)}, bf16[1,192,4096]{2,1,0:T(8,128)(2,1)}, u32[]{:S(2)}) %copy-start.1) | copy-done | bytes 1572888
  3.4 0.0 copy-start.2
  3.5 0.9 %copy-done.2 = bf16[256,256]{1,0:T(8,128)(2,1)S(1)} copy-done((bf16[256,256]{1,0:T(8,128)(2,1)S(1)}, bf16[256,256]{1,0:T(8,128)(2,1)}, u32[]{:S(2)}) %copy-start.2) | copy-done | bytes 131096
  4.4 0.0 copy-start.3
  4.4 0.0 copy-start.4
  4.4 65.1 %grads_and_weights.1 = f32[256,128]{1,0:T(8,128)S(1)} custom-call(bf16[192,4096]{1,0:T(8,128)(2,1)S(1)} %bitcast.2, bf16[192,4096]{1,0:T(8,128)(2,1)S(1)} %bitcast.3, bf16[256,256]{1,0:T(8,128)(2,1)S(1)} %copy-done.2), custom_call_target="tpu_custom_call" | custom-call | tf_op jit(solution)/shard_map/grads_and_weights/pallas_call | solution.py:331
  69.5 0.0 copy-done.3
  69.5 0.0 copy-done.4
  69.5 0.8 %add_divide_fusion = (f32[256,128]{1,0:T(8,128)}, f32[256,128]{1,0:T(8,128)}, f32[256,128]{1,0:T(8,128)}) fusion(f32[256,128]{1,0:T(8,128)S(1)} %grads_and_weights.1, f32[256,128]{1,0:T(8,128)S(1)} %copy-done.3, f32[256,128]{1,0:T(8,128)S(1)} %copy-done.4), kind=kLoop, calls=%fused_computation.2 | loop fusion | flops 360448 | bytes 786432 | tf_op jit(solution)/shard_map/div | solution.py:47
Async XLA Ops:
  0.6 1.4 %copy-start = (bf16[1,192,4096]{2,1,0:T(8,128)(2,1)S(1)}, bf16[1,192,4096]{2,1,0:T(8,128)(2,1)}, u32[]{:S(2)}) copy-start(bf16[1,192,4096]{2,1,0:T(8,128)(2,1)} %param.5) | copy-start | bytes 4718596
  2.0 1.4 %copy-start.1 = (bf16[1,192,4096]{2,1,0:T(8,128)(2,1)S(1)}, bf16[1,192,4096]{2,1,0:T(8,128)(2,1)}, u32[]{:S(2)}) copy-start(bf16[1,192,4096]{2,1,0:T(8,128)(2,1)} %param.6) | copy-start | bytes 4718596
  3.4 0.9 %copy-start.2 = (bf16[256,256]{1,0:T(8,128)(2,1)S(1)}, bf16[256,256]{1,0:T(8,128)(2,1)}, u32[]{:S(2)}) copy-start(bf16[256,256]{1,0:T(8,128)(2,1)} %ada_hbm.1) | copy-start | bytes 393220
  4.4 65.1 %copy-start.3 = (f32[256,128]{1,0:T(8,128)S(1)}, f32[256,128]{1,0:T(8,128)}, u32[]{:S(2)}) copy-start(f32[256,128]{1,0:T(8,128)} %param.9) | copy-start | bytes 393220
  4.4 65.1 %copy-start.4 = (f32[256,128]{1,0:T(8,128)S(1)}, f32[256,128]{1,0:T(8,128)}, u32[]{:S(2)}) copy-start(f32[256,128]{1,0:T(8,128)} %param.8) | copy-start | bytes 393220

commit v3 on v2

--- a/solution.py
+++ b/solution.py
@@ -92,7 +92,7 @@
 def kernel(
     ctx_hbm, cot_hbm, ada_hbm, out,
     ctx, cot,
-    gathered, grad, core_in, x_in, z_in, y_in, gram_out, gram_in, gram_mid, gram_last,
+    gathered, grad, core_in, x_in, z_in, z_far, y_in, gram_out, gram_in, gram_mid, gram_last,
     load, az_s, az_r, ax_s, ax_r, ay_s, ay_r, ac_s, ac_r,
     gc_s, gc_r, gx_s, gx_r, gz_s, gz_r, gy_s, gy_r, ka_s, ka_r, kz_s, kz_r,
 ):
@@ -223,60 +223,162 @@
     low_t = low.T.astype(jnp.bfloat16)
     back_t = back.T.astype(jnp.bfloat16)
 
-    def make(slot):
+    quarter = rank // 2
+    part_a = pl.ds(0, rank)
+    part_u = pl.ds(rank, rank)
+    part_b = pl.ds(rank, quarter)
+    part_q = pl.ds(rank + quarter, quarter)
+    rows_of = (part_a, part_b)
+
+    def make(slot, u):
         cols = columns(slot)
-        grad[slot, :rank, :] = jnp.dot(back_t, ctx[:, cols], preferred_element_type=f32)
-        grad[slot, rank:, :] = jnp.dot(low_t, cot[:, cols], preferred_element_type=f32)
-
-    order = (2, 3, 1, 0)
-
-    def to_core(d, far):
+        if u:
+            grad[slot, part_u, :] = jnp.dot(low_t, cot[:, cols], preferred_element_type=f32)
+        else:
+            grad[slot, part_a, :] = jnp.dot(back_t, ctx[:, cols], preferred_element_type=f32)
+
+    def to_core(d, far, u):
         slot = place(flip2(z, d), 1 - x if far else x, 1 - c)
-        make(slot)
+        make(slot, u)
         k = 4 * far + d
-        go(grad.at[slot], core_in.at[k], gc_s.at[k], gc_r.at[k], cpeer)
-
-    def keep(d, far):
-        make(place(flip2(z, d), 1 - x if far else x, c))
-
-    def add_core(d, far):
-        slot = place(flip2(z, d), 1 - x if far else x, c)
+        part = part_u if u else part_a
+        go(grad.at[slot, part, :], core_in.at[k, part, :], gc_s.at[2 * k + u], gc_r.at[2 * k + u], cpeer)
+
+    def keep(d, far, u):
+        make(line(d, far), u)
+
+    def add_core(d, far, u):
+        slot = line(d, far)
         k = 4 * far + d
-        remote(core_in.at[k], core_in.at[k], gc_s.at[k], gc_r.at[k], cpeer).wait_recv()
-        grad[slot] = grad[slot] + core_in[k]
-        return slot
-
-    def to_x(d):
-        slot = add_core(d, 1)
-        go(grad.at[slot], x_in.at[d], gx_s.at[d], gx_r.at[d], xpeer)
-
-    to_core(order[0], 1)
-    keep(order[0], 1)
-    for before, now in zip(order[:-1], order[1:]):
-        to_core(now, 1)
-        to_x(before)
-        keep(now, 1)
-    to_x(order[-1])
-    for d in order:
-        to_core(d, 0)
-        keep(d, 0)
-    for d in order:
-        slot = add_core(d, 0)
-        remote(x_in.at[d], x_in.at[d], gx_s.at[d], gx_r.at[d], xpeer).wait_recv()
-        grad[slot] = grad[slot] + x_in[d]
-        if d in (1, 2):
-            go(grad.at[slot], z_in.at[d], gz_s.at[d], gz_r.at[d], zpeer[1])
-        if d == 3:
-            remote(z_in.at[2], z_in.at[2], gz_s.at[2], gz_r.at[2], zpeer[1]).wait_recv()
-            grad[slot] = grad[slot] + z_in[2]
-            go(grad.at[slot], z_in.at[0], gz_s.at[3], gz_r.at[3], zpeer[3])
-    remote(z_in.at[1], z_in.at[1], gz_s.at[1], gz_r.at[1], zpeer[1]).wait_recv()
-    remote(z_in.at[0], z_in.at[0], gz_s.at[3], gz_r.at[3], zpeer[3]).wait_recv()
+        part = part_u if u else part_a
+        ref = core_in.at[k, part, :]
+        remote(ref, ref, gc_s.at[2 * k + u], gc_r.at[2 * k + u], cpeer).wait_recv()
+        grad[slot, part, :] = grad[slot, part, :] + core_in[k, part, :]
+
+    def to_x(d, b):
+        part = rows_of[b]
+        go(grad.at[line(d, 1), part, :], x_in.at[d, part, :], gx_s.at[2 * d + b], gx_r.at[2 * d + b], xpeer)
+
+    def from_x(d, b):
+        part = rows_of[b]
+        ref = x_in.at[d, part, :]
+        remote(ref, ref, gx_s.at[2 * d + b], gx_r.at[2 * d + b], xpeer).wait_recv()
+        grad[line(d, 0), part, :] = grad[line(d, 0), part, :] + x_in[d, part, :]
+
+    def z_ref(m, chunk):
+        if chunk == 3:
+            return z_far.at[m]
+        return z_in.at[m, (part_a, part_b, part_q)[chunk], :]
+
+    def grad_ref(d, chunk):
+        return grad.at[line(d, chunk == 3), (part_a, part_b, part_q, part_q)[chunk], :]
+
+    def to_z(d, chunk):
+        m = 0 if d == 3 else d
+        n = 4 * m + chunk
+        go(grad_ref(d, chunk), z_ref(m, chunk), gz_s.at[n], gz_r.at[n], zpeer[3 if d == 3 else 1])
+
+    def from_z_sum(m, chunk):
+        n = 4 * m + chunk
+        ref = z_ref(m, chunk)
+        remote(ref, ref, gz_s.at[n], gz_r.at[n], zpeer[1 if m else 3]).wait_recv()
+        into = grad_ref(3 if m == 2 else 0, chunk)
+        into[...] = into[...] + ref[...]
+
+    to_core(2, 1, 0)
+    keep(2, 1, 0)
+    to_core(3, 1, 0)
+    add_core(2, 1, 0)
+    to_x(2, 0)
+    keep(3, 1, 0)
+    to_core(2, 1, 1)
+    add_core(3, 1, 0)
+    to_x(3, 0)
+    keep(2, 1, 1)
+    to_core(1, 1, 1)
+    add_core(2, 1, 1)
+    to_z(2, 3)
+    to_x(2, 1)
+    keep(1, 1, 1)
+    to_core(2, 0, 1)
+    add_core(1, 1, 1)
+    keep(2, 0, 1)
+    to_core(3, 1, 1)
+    add_core(2, 0, 1)
+    to_z(2, 2)
+    to_z(1, 3)
+    keep(3, 1, 1)
+    to_core(1, 0, 1)
+    add_core(3, 1, 1)
+    to_x(3, 1)
+    keep(1, 0, 1)
+    to_core(1, 1, 0)
+    add_core(1, 0, 1)
+    to_z(1, 2)
+    keep(1, 1, 0)
+    to_core(2, 0, 0)
+    add_core(1, 1, 0)
+    to_x(1, 0)
+    to_x(1, 1)
+    keep(2, 0, 0)
+    to_core(3, 0, 0)
+    add_core(2, 0, 0)
+    from_x(2, 0)
+    to_z(2, 0)
+    keep(3, 0, 0)
+    to_core(3, 0, 1)
+    keep(3, 0, 1)
+    to_core(0, 1, 0)
+    keep(0, 1, 0)
+    to_core(0, 1, 1)
+    add_core(0, 1, 0)
+    to_x(0, 0)
+    keep(0, 1, 1)
+    add_core(3, 0, 0)
+    add_core(3, 0, 1)
+    add_core(0, 1, 1)
+    to_x(0, 1)
+    from_z_sum(2, 3)
+    to_z(3, 3)
+    from_z_sum(2, 2)
+    to_z(3, 2)
+    from_x(2, 1)
+    to_z(2, 1)
+    from_x(3, 0)
+    to_core(1, 0, 0)
+    keep(1, 0, 0)
+    to_core(0, 0, 0)
+    keep(0, 0, 0)
+    to_core(0, 0, 1)
+    keep(0, 0, 1)
+    from_z_sum(2, 0)
+    to_z(3, 0)
+    add_core(1, 0, 0)
+    add_core(0, 0, 0)
+    add_core(0, 0, 1)
+    from_x(3, 1)
+    from_z_sum(2, 1)
+    to_z(3, 1)
+    from_x(1, 0)
+    to_z(1, 0)
+    from_z_sum(1, 3)
+    from_z_sum(0, 3)
+    go(grad_ref(0, 3), x_in.at[0, part_q, :], gx_s.at[8], gx_r.at[8], xpeer)
+    from_x(1, 1)
+    to_z(1, 1)
+    from_z_sum(1, 2)
+    from_z_sum(0, 2)
+    for b in (0, 1):
+        from_x(0, b)
+    for m in (0, 1):
+        for b in (0, 1):
+            from_z_sum(m, b)
+    remote(x_in.at[0, part_q, :], x_in.at[0, part_q, :], gx_s.at[8], gx_r.at[8], xpeer).wait_recv()
+    grad[f, part_q, :] = grad[f, part_q, :] + x_in[0, part_q, :]
     mine = pl.ds(pl.multiple_of(t * rank, rank), rank)
     theirs = pl.ds(pl.multiple_of((1 - t) * rank, rank), rank)
-    z_in[0, theirs, :] = grad[f, theirs, :] + z_in[0, theirs, :] + z_in[1, theirs, :]
-    go(z_in.at[0, theirs, :], y_in, gy_s, gy_r, cube[4])
-    own = grad[f, mine, :] + z_in[0, mine, :] + z_in[1, mine, :]
+    go(grad.at[f, theirs, :], y_in, gy_s, gy_r, cube[4])
+    own = grad[f, mine, :]
     remote(y_in, y_in, gy_s, gy_r, cube[4]).wait_recv()
     other = y_in[...]
 
@@ -341,13 +443,14 @@
             pltpu.VMEM((8, width, rows), f32),
             pltpu.VMEM((4, width, rows), f32),
             pltpu.VMEM((3, width, rows), f32),
+            pltpu.VMEM((3, rank // 2, rows), f32),
             pltpu.VMEM((rank, rows), f32),
             pltpu.VMEM((8, 128), f32),
             pltpu.VMEM((8, 8, 128), f32),
             pltpu.VMEM((8, 128), f32),
             pltpu.VMEM((4, 8, 128), f32),
             dma((3,)), dma((4,)), dma((4,)), dma((4,)), dma((4,)), dma((8,)), dma((8,)), dma((16,)), dma((16,)),
-            dma((8,)), dma((8,)), dma((4,)), dma((4,)), dma((4,)), dma((4,)),
+            dma((16,)), dma((16,)), dma((9,)), dma((9,)), dma((12,)), dma((12,)),
             dma, dma, dma((8,)), dma((8,)), dma((4,)), dma((4,)),
         ],
         compiler_params=pltpu.CompilerParams(

time: 70.5 us -> 67.7 us (0.960)
  Pallas kernels: 65.1 us -> 62.3 us
    pallas_call x1, Pallas kernels: 65.1 us -> 62.3 us  [kernel_body(): pl.pallas_call(kernel, out_shape=jax.ShapeDtypeStruct((rows, rank), f32),...]
where the time goes in v3:
time: 67.7 us; the launch traced here: 67.5 us
  Pallas kernels  62.3 us (92%)
  local copies, waits for them, and re-layouts  3.72 us (5%)
  other arithmetic  0.78 us (1%)
    pallas_call x1, Pallas kernels, kernel_body(): pl.pallas_call(kernel, out_shape=jax.ShapeDtypeStruct((rows, rank), f32),...  62.3 us
    unnamed x10, local copies, waits for them, and re-layouts  3.72 us

profile of v3, /device:TPU:0, one launch (start us, length us, event | category | flops | bytes accessed | tf_op | source)
XLA Modules:
  0.0 67.5 jit_solution(13999295066010837879)
XLA Ops:
  0.6 0.0 copy-start
  0.6 1.4 %copy-done = bf16[1,192,4096]{2,1,0:T(8,128)(2,1)S(1)} copy-done((bf16[1,192,4096]{2,1,0:T(8,128)(2,1)S(1)}, bf16[1,192,4096]{2,1,0:T(8,128)(2,1)}, u32[]{:S(2)}) %copy-start) | copy-done | bytes 1572888
  2.0 0.0 copy-start.1
  2.0 1.4 %copy-done.1 = bf16[1,192,4096]{2,1,0:T(8,128)(2,1)S(1)} copy-done((bf16[1,192,4096]{2,1,0:T(8,128)(2,1)S(1)}, bf16[1,192,4096]{2,1,0:T(8,128)(2,1)}, u32[]{:S(2)}) %copy-start.1) | copy-done | bytes 1572888
  3.4 0.0 copy-start.2
  3.5 0.9 %copy-done.2 = bf16[256,256]{1,0:T(8,128)(2,1)S(1)} copy-done((bf16[256,256]{1,0:T(8,128)(2,1)S(1)}, bf16[256,256]{1,0:T(8,128)(2,1)}, u32[]{:S(2)}) %copy-start.2) | copy-done | bytes 131096
  4.4 0.0 copy-start.3
  4.4 0.0 copy-start.4
  4.4 62.3 %grads_and_weights.1 = f32[256,128]{1,0:T(8,128)S(1)} custom-call(bf16[192,4096]{1,0:T(8,128)(2,1)S(1)} %bitcast.2, bf16[192,4096]{1,0:T(8,128)(2,1)S(1)} %bitcast.3, bf16[256,256]{1,0:T(8,128)(2,1)S(1)} %copy-done.2), custom_call_target="tpu_custom_call" | custom-call | tf_op jit(solution)/shard_map/grads_and_weights/pallas_call | solution.py:433
  66.7 0.0 copy-done.3
  66.7 0.0 copy-done.4
  66.7 0.8 %add_divide_fusion = (f32[256,128]{1,0:T(8,128)}, f32[256,128]{1,0:T(8,128)}, f32[256,128]{1,0:T(8,128)}) fusion(f32[256,128]{1,0:T(8,128)S(1)} %grads_and_weights.1, f32[256,128]{1,0:T(8,128)S(1)} %copy-done.3, f32[256,128]{1,0:T(8,128)S(1)} %copy-done.4), kind=kLoop, calls=%fused_computation.2 | loop fusion | flops 360448 | bytes 786432 | tf_op jit(solution)/shard_map/div | solution.py:47
Async XLA Ops:
  0.6 1.4 %copy-start = (bf16[1,192,4096]{2,1,0:T(8,128)(2,1)S(1)}, bf16[1,192,4096]{2,1,0:T(8,128)(2,1)}, u32[]{:S(2)}) copy-start(bf16[1,192,4096]{2,1,0:T(8,128)(2,1)} %param.5) | copy-start | bytes 4718596
  2.0 1.4 %copy-start.1 = (bf16[1,192,4096]{2,1,0:T(8,128)(2,1)S(1)}, bf16[1,192,4096]{2,1,0:T(8,128)(2,1)}, u32[]{:S(2)}) copy-start(bf16[1,192,4096]{2,1,0:T(8,128)(2,1)} %param.6) | copy-start | bytes 4718596
  3.4 0.9 %copy-start.2 = (bf16[256,256]{1,0:T(8,128)(2,1)S(1)}, bf16[256,256]{1,0:T(8,128)(2,1)}, u32[]{:S(2)}) copy-start(bf16[256,256]{1,0:T(8,128)(2,1)} %ada_hbm.1) | copy-start | bytes 393220
  4.4 62.3 %copy-start.3 = (f32[256,128]{1,0:T(8,128)S(1)}, f32[256,128]{1,0:T(8,128)}, u32[]{:S(2)}) copy-start(f32[256,128]{1,0:T(8,128)} %param.9) | copy-start | bytes 393220
  4.4 62.3 %copy-start.4 = (f32[256,128]{1,0:T(8,128)S(1)}, f32[256,128]{1,0:T(8,128)}, u32[]{:S(2)}) copy-start(f32[256,128]{1,0:T(8,128)} %param.8) | copy-start | bytes 393220

commit v4 on v3

--- a/solution.py
+++ b/solution.py
@@ -175,7 +175,7 @@
         move_block(slot, part, ac_s.at[k], ac_r.at[k], cpeer)
 
     loads[0].wait()
-    for d in (3, 2, 1):
+    for d in (1, 2, 3):
         move_block(f, near_half, az_s.at[d], az_r.at[d], zpeer[d])
     move_block(f, whole, ax_s.at[0], ax_r.at[0], xpeer)
     to_other_core(f, whole, 0)

time: 67.7 us -> 66.7 us (0.985)
  Pallas kernels: 62.3 us -> 61.4 us
    pallas_call x1, Pallas kernels: 62.3 us -> 61.4 us  [kernel_body(): pl.pallas_call(kernel, out_shape=jax.ShapeDtypeStruct((rows, rank), f32),...]
where the time goes in v4:
time: 66.7 us; the launch traced here: 66.5 us
  Pallas kernels  61.4 us (92%)
  local copies, waits for them, and re-layouts  3.72 us (6%)
  other arithmetic  0.78 us (1%)
  between operations  0.67 us (1%)
    pallas_call x1, Pallas kernels, kernel_body(): pl.pallas_call(kernel, out_shape=jax.ShapeDtypeStruct((rows, rank), f32),...  61.4 us
    unnamed x10, local copies, waits for them, and re-layouts  3.72 us

profile of v4, /device:TPU:0, one launch (start us, length us, event | category | flops | bytes accessed | tf_op | source)
XLA Modules:
  0.0 66.5 jit_solution(10085664975147287574)
XLA Ops:
  0.6 0.0 copy-start
  0.6 1.4 %copy-done = bf16[1,192,4096]{2,1,0:T(8,128)(2,1)S(1)} copy-done((bf16[1,192,4096]{2,1,0:T(8,128)(2,1)S(1)}, bf16[1,192,4096]{2,1,0:T(8,128)(2,1)}, u32[]{:S(2)}) %copy-start) | copy-done | bytes 1572888
  2.0 0.0 copy-start.1
  2.0 1.4 %copy-done.1 = bf16[1,192,4096]{2,1,0:T(8,128)(2,1)S(1)} copy-done((bf16[1,192,4096]{2,1,0:T(8,128)(2,1)S(1)}, bf16[1,192,4096]{2,1,0:T(8,128)(2,1)}, u32[]{:S(2)}) %copy-start.1) | copy-done | bytes 1572888
  3.4 0.0 copy-start.2
  3.5 0.9 %copy-done.2 = bf16[256,256]{1,0:T(8,128)(2,1)S(1)} copy-done((bf16[256,256]{1,0:T(8,128)(2,1)S(1)}, bf16[256,256]{1,0:T(8,128)(2,1)}, u32[]{:S(2)}) %copy-start.2) | copy-done | bytes 131096
  4.4 0.0 copy-start.3
  4.4 0.0 copy-start.4
  4.4 61.4 %grads_and_weights.1 = f32[256,128]{1,0:T(8,128)S(1)} custom-call(bf16[192,4096]{1,0:T(8,128)(2,1)S(1)} %bitcast.2, bf16[192,4096]{1,0:T(8,128)(2,1)S(1)} %bitcast.3, bf16[256,256]{1,0:T(8,128)(2,1)S(1)} %copy-done.2), custom_call_target="tpu_custom_call" | custom-call | tf_op jit(solution)/shard_map/grads_and_weights/pallas_call | solution.py:433
  65.7 0.0 copy-done.3
  65.7 0.0 copy-done.4
  65.7 0.8 %add_divide_fusion = (f32[256,128]{1,0:T(8,128)}, f32[256,128]{1,0:T(8,128)}, f32[256,128]{1,0:T(8,128)}) fusion(f32[256,128]{1,0:T(8,128)S(1)} %grads_and_weights.1, f32[256,128]{1,0:T(8,128)S(1)} %copy-done.3, f32[256,128]{1,0:T(8,128)S(1)} %copy-done.4), kind=kLoop, calls=%fused_computation.2 | loop fusion | flops 360448 | bytes 786432 | tf_op jit(solution)/shard_map/div | solution.py:47
Async XLA Ops:
  0.6 1.4 %copy-start = (bf16[1,192,4096]{2,1,0:T(8,128)(2,1)S(1)}, bf16[1,192,4096]{2,1,0:T(8,128)(2,1)}, u32[]{:S(2)}) copy-start(bf16[1,192,4096]{2,1,0:T(8,128)(2,1)} %param.5) | copy-start | bytes 4718596
  2.0 1.4 %copy-start.1 = (bf16[1,192,4096]{2,1,0:T(8,128)(2,1)S(1)}, bf16[1,192,4096]{2,1,0:T(8,128)(2,1)}, u32[]{:S(2)}) copy-start(bf16[1,192,4096]{2,1,0:T(8,128)(2,1)} %param.6) | copy-start | bytes 4718596
  3.4 0.9 %copy-start.2 = (bf16[256,256]{1,0:T(8,128)(2,1)S(1)}, bf16[256,256]{1,0:T(8,128)(2,1)}, u32[]{:S(2)}) copy-start(bf16[256,256]{1,0:T(8,128)(2,1)} %ada_hbm.1) | copy-start | bytes 393220
  4.4 61.4 %copy-start.3 = (f32[256,128]{1,0:T(8,128)S(1)}, f32[256,128]{1,0:T(8,128)}, u32[]{:S(2)}) copy-start(f32[256,128]{1,0:T(8,128)} %param.9) | copy-start | bytes 393220
  4.4 61.4 %copy-start.4 = (f32[256,128]{1,0:T(8,128)S(1)}, f32[256,128]{1,0:T(8,128)}, u32[]{:S(2)}) copy-start(f32[256,128]{1,0:T(8,128)} %param.8) | copy-start | bytes 393220

commit v5 on v4

--- a/solution.py
+++ b/solution.py
@@ -211,7 +211,9 @@
             slot = line(d, far)
             await_block(slot, far_half, ay_s.at[k], ay_r.at[k], ypeer)
             to_other_core(slot, far_half, 8 + k)
-            low, back = consume(slot, low, back)
+    for far in (0, 1):
+        for d in (1, 2, 3):
+            low, back = consume(line(d, far), low, back)
     for far in (0, 1):
         for d in (1, 2, 3):
             k = 4 * far + d

time: 66.7 us -> 67 us (level)
  no operation moved by 1% of the time
where the time goes in v5:
time: 67 us; the launch traced here: 66.8 us
  Pallas kernels  61.7 us (92%)
  local copies, waits for them, and re-layouts  3.72 us (6%)
  other arithmetic  0.78 us (1%)
  between operations  0.67 us (1%)
    pallas_call x1, Pallas kernels, kernel_body(): pl.pallas_call(kernel, out_shape=jax.ShapeDtypeStruct((rows, rank), f32),...  61.7 us
    unnamed x10, local copies, waits for them, and re-layouts  3.72 us

profile of v5, /device:TPU:0, one launch (start us, length us, event | category | flops | bytes accessed | tf_op | source)
XLA Modules:
  0.0 66.8 jit_solution(6909216716642364146)
XLA Ops:
  0.6 0.0 copy-start
  0.6 1.4 %copy-done = bf16[1,192,4096]{2,1,0:T(8,128)(2,1)S(1)} copy-done((bf16[1,192,4096]{2,1,0:T(8,128)(2,1)S(1)}, bf16[1,192,4096]{2,1,0:T(8,128)(2,1)}, u32[]{:S(2)}) %copy-start) | copy-done | bytes 1572888
  2.0 0.0 copy-start.1
  2.0 1.4 %copy-done.1 = bf16[1,192,4096]{2,1,0:T(8,128)(2,1)S(1)} copy-done((bf16[1,192,4096]{2,1,0:T(8,128)(2,1)S(1)}, bf16[1,192,4096]{2,1,0:T(8,128)(2,1)}, u32[]{:S(2)}) %copy-start.1) | copy-done | bytes 1572888
  3.4 0.0 copy-start.2
  3.5 0.9 %copy-done.2 = bf16[256,256]{1,0:T(8,128)(2,1)S(1)} copy-done((bf16[256,256]{1,0:T(8,128)(2,1)S(1)}, bf16[256,256]{1,0:T(8,128)(2,1)}, u32[]{:S(2)}) %copy-start.2) | copy-done | bytes 131096
  4.4 0.0 copy-start.3
  4.4 0.0 copy-start.4
  4.4 61.7 %grads_and_weights.1 = f32[256,128]{1,0:T(8,128)S(1)} custom-call(bf16[192,4096]{1,0:T(8,128)(2,1)S(1)} %bitcast.2, bf16[192,4096]{1,0:T(8,128)(2,1)S(1)} %bitcast.3, bf16[256,256]{1,0:T(8,128)(2,1)S(1)} %copy-done.2), custom_call_target="tpu_custom_call" | custom-call | tf_op jit(solution)/shard_map/grads_and_weights/pallas_call | solution.py:435
  66.0 0.0 copy-done.3
  66.0 0.0 copy-done.4
  66.0 0.8 %add_divide_fusion = (f32[256,128]{1,0:T(8,128)}, f32[256,128]{1,0:T(8,128)}, f32[256,128]{1,0:T(8,128)}) fusion(f32[256,128]{1,0:T(8,128)S(1)} %grads_and_weights.1, f32[256,128]{1,0:T(8,128)S(1)} %copy-done.3, f32[256,128]{1,0:T(8,128)S(1)} %copy-done.4), kind=kLoop, calls=%fused_computation.2 | loop fusion | flops 360448 | bytes 786432 | tf_op jit(solution)/shard_map/div | solution.py:47
Async XLA Ops:
  0.6 1.4 %copy-start = (bf16[1,192,4096]{2,1,0:T(8,128)(2,1)S(1)}, bf16[1,192,4096]{2,1,0:T(8,128)(2,1)}, u32[]{:S(2)}) copy-start(bf16[1,192,4096]{2,1,0:T(8,128)(2,1)} %param.5) | copy-start | bytes 4718596
  2.0 1.4 %copy-start.1 = (bf16[1,192,4096]{2,1,0:T(8,128)(2,1)S(1)}, bf16[1,192,4096]{2,1,0:T(8,128)(2,1)}, u32[]{:S(2)}) copy-start(bf16[1,192,4096]{2,1,0:T(8,128)(2,1)} %param.6) | copy-start | bytes 4718596
  3.4 0.9 %copy-start.2 = (bf16[256,256]{1,0:T(8,128)(2,1)S(1)}, bf16[256,256]{1,0:T(8,128)(2,1)}, u32[]{:S(2)}) copy-start(bf16[256,256]{1,0:T(8,128)(2,1)} %ada_hbm.1) | copy-start | bytes 393220
  4.4 61.7 %copy-start.3 = (f32[256,128]{1,0:T(8,128)S(1)}, f32[256,128]{1,0:T(8,128)}, u32[]{:S(2)}) copy-start(f32[256,128]{1,0:T(8,128)} %param.9) | copy-start | bytes 393220
  4.4 61.7 %copy-start.4 = (f32[256,128]{1,0:T(8,128)S(1)}, f32[256,128]{1,0:T(8,128)}, u32[]{:S(2)}) copy-start(f32[256,128]{1,0:T(8,128)} %param.8) | copy-start | bytes 393220
